TPU v7x, 256 devices: a whole 4x4x8 slice. The times are simulated.
256 devices in a mesh: ctx: 64 (over x, y_lo, z), ch: 4 (over y_hi, core).
Axes of the slice: x: 4, y: 4 (y_hi: 2, y_lo: 2; y = y_hi * 2 + y_lo), z: 8, core: 2. Of those that a mesh axis runs over, the one named last changes fastest.
Arguments:
- token_ids: int32 [8192], P('ctx'), may hold values from 0 to 511
- tables: bfloat16 [512, 3, 8192], P(None, None, 'ch'), may hold values from -6 to 6
- filter_long: bfloat16 [8192, 8192], P('ctx', 'ch'), may hold values from -0.0625 to 0.0625
- skip_long: float32 [8192], P('ch'), may hold values from -4 to 4
- taps_in: float32 [3, 3, 8192], P(None, None, 'ch'), may hold values from -3 to 3
- projection: bfloat16 [8192, 3, 1024], P('ch', None, 'ctx'), may hold values from -0.0625 to 0.0625
- taps_proj: float32 [3, 3, 1024], P(None, None, 'ch'), may hold values from -3 to 3
- taps_short: float32 [7, 1024], P(None, 'ch'), may hold values from -2 to 2
- skip_short: float32 [1024], P('ch'), may hold values from -4 to 4
Outputs:
- mixed_out: bfloat16 [8192, 1024], P('ctx', 'ch')
All inputs are finite; a program needn't handle non-finite values.
Results may differ from a plain program's by a relative error of at most 0.025.
Values may be sent and summed in bfloat16 or wider, within the bound.
A program may use at most 128 MiB of HBM per device.

v0:
```python
import jax
import jax.numpy as jnp
from jax import lax
from jax.sharding import PartitionSpec as P

radix_rows = 256
precise = lax.Precision.HIGH


def from_behind(value, axis, steps):
    count = lax.axis_size(axis)
    initial, last = (max(0, -steps), min(count, count - steps))
    return lax.ppermute(value, axis, [(source, source + steps) for source in range(initial, last)])


def short_filter(extended, taps):
    span = taps.shape[0]
    count = extended.shape[0] - span + 1
    total = taps[0] * extended[span - 1 : span - 1 + count]
    for offset in range(1, span):
        total = total + taps[offset] * extended[span - 1 - offset : span - 1 - offset + count]
    return total


def angle_table(first, second, modulus):
    left = jnp.arange(first, dtype=jnp.int32)[:, None]
    right = jnp.arange(second, dtype=jnp.int32)[None, :]
    phase = (left * right % modulus).astype(jnp.float32) * (2.0 * jnp.pi / modulus)
    return (jnp.cos(phase), jnp.sin(phase))


def forward(signal, cos_one, sin_one, cos_tw, sin_tw, cos_two, sin_two):
    part_re = jnp.einsum("kn,mnb->mkb", cos_one, signal, precision=precise)
    part_im = -jnp.einsum("kn,mnb->mkb", sin_one, signal, precision=precise)
    turned_re = part_re * cos_tw + part_im * sin_tw
    turned_im = part_im * cos_tw - part_re * sin_tw
    out_re = jnp.einsum("mkb,bj->mkj", turned_re, cos_two, precision=precise) + jnp.einsum(
        "mkb,bj->mkj", turned_im, sin_two, precision=precise
    )
    out_im = jnp.einsum("mkb,bj->mkj", turned_im, cos_two, precision=precise) - jnp.einsum(
        "mkb,bj->mkj", turned_re, sin_two, precision=precise
    )
    return (out_re, out_im)


def convolve(pair):
    gated, filt = pair
    seq_len, items, width = gated.shape
    total_len = 2 * seq_len
    second = total_len // radix_rows
    half = radix_rows // 2
    channels = items * width
    cos_one, sin_one = angle_table(radix_rows, half, radix_rows)
    cos_tw, sin_tw = angle_table(radix_rows, second, total_len)
    cos_two, sin_two = angle_table(second, second, second)

    def prepare(array):
        return jnp.transpose(array.astype(jnp.float32), (1, 2, 0)).reshape(channels, half, second)

    sig_re, sig_im = forward(prepare(gated), cos_one, sin_one, cos_tw, sin_tw, cos_two, sin_two)
    fil_re, fil_im = forward(prepare(filt), cos_one, sin_one, cos_tw, sin_tw, cos_two, sin_two)
    prod_re = sig_re * fil_re - sig_im * fil_im
    prod_im = sig_re * fil_im + sig_im * fil_re
    back_re = jnp.einsum("mkj,bj->mkb", prod_re, cos_two, precision=precise) - jnp.einsum(
        "mkj,bj->mkb", prod_im, sin_two, precision=precise
    )
    back_im = jnp.einsum("mkj,bj->mkb", prod_im, cos_two, precision=precise) + jnp.einsum(
        "mkj,bj->mkb", prod_re, sin_two, precision=precise
    )
    turn_re = back_re * cos_tw - back_im * sin_tw
    turn_im = back_im * cos_tw + back_re * sin_tw
    result = jnp.einsum("kn,mkb->mnb", cos_one, turn_re, precision=precise) - jnp.einsum(
        "kn,mkb->mnb", sin_one, turn_im, precision=precise
    )
    result = result * (1.0 / total_len)
    result = jnp.transpose(result.reshape(items, width, seq_len), (2, 0, 1))
    return result.astype(jnp.bfloat16)


def per_device(
    token_ids,
    tables,
    filter_long,
    skip_long,
    taps_in,
    projection,
    taps_proj,
    taps_short,
    skip_short,
):
    token_rows = token_ids.shape[0]
    vocab_size, triple, width_dev = tables.shape
    onehot = (token_ids[:, None] == jnp.arange(vocab_size, dtype=jnp.int32)[None, :]).astype(
        jnp.bfloat16
    )
    embedded = jnp.dot(
        onehot, tables.reshape(vocab_size, triple * width_dev), preferred_element_type=jnp.float32
    )
    embedded = embedded.astype(jnp.bfloat16).reshape(token_rows, triple, width_dev)
    before = from_behind(embedded[token_rows - 2 :], "ctx", 1)
    features = short_filter(jnp.concatenate([before, embedded], 0).astype(jnp.float32), taps_in)
    query_one = features[:, 0]
    gated_one = (features[:, 1] * features[:, 2]).astype(jnp.bfloat16)
    grouped = (
        gated_one.reshape(token_rows, 2, width_dev // 2),
        filter_long.reshape(token_rows, 2, width_dev // 2),
    )
    moved = (
        lax.all_to_all(grouped[0], "ctx", split_axis=2, concat_axis=0, tiled=True),
        lax.all_to_all(grouped[1], "ctx", split_axis=2, concat_axis=0, tiled=True),
    )
    long_one = lax.all_to_all(convolve(moved), "ctx", split_axis=0, concat_axis=2, tiled=True)
    long_one = long_one.reshape(token_rows, width_dev)
    layer_one = (
        query_one * (long_one.astype(jnp.float32) + skip_long * gated_one.astype(jnp.float32))
    ).astype(jnp.bfloat16)
    partial_sums = jnp.einsum(
        "te,ejc->tjc",
        layer_one,
        lax.all_gather(projection, "ctx", axis=2, tiled=True),
        preferred_element_type=jnp.float32,
    )
    summed = lax.psum_scatter(partial_sums, "ch", scatter_dimension=2, tiled=True)
    projected = summed.astype(jnp.bfloat16)
    earlier = from_behind(projected[token_rows - 2 :], "ctx", 1)
    feat_two = short_filter(jnp.concatenate([earlier, projected], 0).astype(jnp.float32), taps_proj)
    query_two = feat_two[:, 0]
    gated_two = feat_two[:, 1] * feat_two[:, 2]
    prior_gated = from_behind(gated_two[token_rows - 6 :], "ctx", 1)
    short_two = short_filter(jnp.concatenate([prior_gated, gated_two], 0), taps_short)
    return (query_two * (short_two + skip_short * gated_two)).astype(jnp.bfloat16)


def solution(mesh):
    placed = (
        P("ctx"),
        P(None, None, "ch"),
        P("ctx", "ch"),
        P("ch"),
        P(None, None, "ch"),
        P("ch", None, "ctx"),
        P(None, None, "ch"),
        P(None, "ch"),
        P("ch"),
    )
    return jax.shard_map(
        per_device, mesh=mesh, in_specs=placed, out_specs=P("ctx", "ch"), check_vma=False
    )
```

profile of v0, /device:TPU:6, one launch (start us, length us, event | category | flops | bytes accessed | tf_op | source)
XLA Modules:
  0.0 418.1 jit_solution(14183931414274058860)
XLA Ops:
  7.3 8.7 %copy.93 = bf16[512,3,2048]{0,2,1:T(8,128)(2,1)} copy(bf16[512,3,2048]{2,0,1:T(8,128)(2,1)} %param.10) | data formatting | bytes 12582912 | tf_op args[1]
  16.0 5.0 %convolution_convert_fusion = bf16[128,6144]{1,0:T(8,128)(2,1)S(1)} fusion(bf16[512,6144]{0,1:T(8,128)(2,1)} %bitcast.187, s32[128]{0:T(128)S(1)} %copy-done.9), kind=kOutput, calls=%fused_computation | convolution fusion | flops 806158336 | bytes 7864832 | tf_op jit(solution)/shard_map/dot_general | solution.py:96
  21.1 3.8 collective-permute-start
  26.5 12.5 %all-to-all-start.1 = ((bf16[128,2,1024]{0,1,2:T(2,128)(2,1)}), bf16[128,2,1024]{0,1,2:T(2,128)(2,1)}, u32[]{:S(2)}, u32[]{:S(2)}) async-start(bf16[128,2,1024]{0,1,2:T(2,128)(2,1)} %copy.104), calls=%async_computation.1 | async-start | bytes 1048576 | tf_op jit(solution)/shard_map/all_to_all | solution.py:110
  42.2 4.7 %fusion = f32[128,3,2048]{0,2,1:T(8,128)S(1)} fusion(f32[130,3,2048]{0,2,1:T(8,128)S(1)} %maximum_convert_fusion, f32[3,2048]{1,0:T(4,128)S(1)} %get-tuple-element.8, f32[3,2048]{1,0:T(4,128)S(1)} %get-tuple-element.9, f32[3,2048]{1,0:T(4,128)S(1)} %get-tuple-element.7), kind=kLoop, calls=%fused_computation.2 | loop fusion | flops 3932160 | bytes 12656640 | tf_op jit(solution)/shard_map/add | solution.py:21
  48.4 11.4 %all-to-all-done.1 = bf16[128,2,1024]{0,1,2:T(2,128)(2,1)} async-done(((bf16[128,2,1024]{0,1,2:T(2,128)(2,1)}), bf16[128,2,1024]{0,1,2:T(2,128)(2,1)}, u32[]{:S(2)}, u32[]{:S(2)}) %all-to-all-start.1) | async-done | bytes 524320 | tf_op jit(solution)/shard_map/all_to_all | solution.py:110
  59.8 8.6 %all-to-all-start = ((bf16[128,2,1024]{0,1,2:T(2,128)(2,1)}), bf16[128,2,1024]{0,1,2:T(2,128)(2,1)}, u32[]{:S(2)}, u32[]{:S(2)}) async-start(bf16[128,2,1024]{0,1,2:T(2,128)(2,1)} %copy.96), calls=%async_computation | async-start | bytes 1048576 | tf_op jit(solution)/shard_map/all_to_all | solution.py:109
  70.7 2.8 reshape.78
  82.2 2.9 fusion.20
  85.1 2.9 fusion.23
  90.8 3.0 reshape.76
  93.8 2.7 fusion.80
  116.5 2.7 convert_element_type.138
  119.2 8.6 %copy.116 = bf16[8192,2,16]{2,1,0:T(2,128)(2,1)} copy(bf16[8192,2,16]{0,2,1:T(8,128)(2,1)} %bitcast.193) | data formatting | bytes 1048576 | tf_op jit(solution)/shard_map/convert_element_type | solution.py:77
  127.8 12.9 %reshape.99 = bf16[64,2,2048]{2,1,0:T(2,128)(2,1)} reshape(bf16[8192,2,16]{2,1,0:T(2,128)(2,1)} %copy.116) | data formatting | bytes 1048576
  140.7 30.8 %all_to_all.45 = bf16[64,2,2048]{2,1,0:T(2,128)(2,1)} all-to-all(bf16[64,2,2048]{2,1,0:T(2,128)(2,1)} %reshape.99), channel_id=1, replica_groups=mesh['ctx'=64,'ch'=4] {'ctx'}, dimensions={0} | all-to-all | bytes 1048576 | tf_op jit(solution)/shard_map/all_to_all | solution.py:112
  171.6 14.1 %reshape.100 = bf16[8192,2,16]{2,1,0:T(2,128)(2,1)} reshape(bf16[64,2,2048]{2,1,0:T(2,128)(2,1)} %all_to_all.45) | data formatting | bytes 1048576
  185.6 8.8 %copy.117 = bf16[8192,2,16]{0,2,1:T(8,128)(2,1)} copy(bf16[8192,2,16]{2,1,0:T(2,128)(2,1)} %reshape.100) | data formatting | bytes 1048576 | tf_op jit(solution)/shard_map/all_to_all | solution.py:112
  197.7 129.1 %all-gather.2.cloned.1.call-done = bf16[2048,3,1024]{0,2,1:T(8,128)(2,1)} async-done(((bf16[2048,3,16]{0,2,1:T(8,128)(2,1)}), bf16[2048,3,1024]{0,2,1:T(8,128)(2,1)}) %all-gather.2.cloned.1.call-update) | async-done | bytes 12582928 | tf_op jit(solution)/shard_map/all_gather | solution.py:120
  326.8 10.3 %fusion.46 = f32[128,3,1024]{2,0,1:T(8,128)} fusion(bf16[2048,3,1024]{0,2,1:T(8,128)(2,1)} %all-gather.2.cloned.1.call-done, bf16[128,2048]{0,1:T(8,128)(2,1)} %fusion.40), kind=kOutput, calls=%fused_computation.56 | convolution fusion | flops 1610612736 | bytes 14680064 | tf_op jit(solution)/shard_map/te,ejc->tjc/dot_general | solution.py:117
  337.1 54.9 %reduce-scatter.2.cloned.1.call-done = f32[128,3,256]{2,0,1:T(8,128)} async-done(((f32[128,3,1024]{2,0,1:T(8,128)}), f32[128,3,256]{2,0,1:T(8,128)}) %reduce-scatter.2.cloned.1.call-update) | async-done | bytes 393232 | tf_op jit(solution)/shard_map/reduce_scatter | solution.py:123
  393.0 3.5 collective-permute-start.1
  396.5 5.0 %collective-permute-done.1 = bf16[2,3,256]{2,0,1:T(2,128)(2,1)S(1)} collective-permute-done((bf16[2,3,256]{2,0,1:T(2,128)(2,1)S(1)}, bf16[2,3,256]{2,0,1:T(2,128)(2,1)S(1)}, u32[]{:S(2)}, u32[]{:S(2)}) %collective-permute-start.1) | collective-permute-done | bytes 3104 | tf_op jit(solution)/shard_map/ppermute | solution.py:13
  403.7 6.6 %collective-permute-done.2 = f32[6,256]{1,0:T(8,128)S(1)} collective-permute-done((f32[6,256]{1,0:T(8,128)S(1)}, f32[6,256]{1,0:T(8,128)S(1)}, u32[]{:S(2)}, u32[]{:S(2)}) %collective-permute-start.2) | collective-permute-done | bytes 6176 | tf_op jit(solution)/shard_map/ppermute | solution.py:13
  (75 shorter events, 47.8 us)
Async XLA Ops:
  6.5 320.2 %all-gather.2.cloned.1.call-start = ((), (), s32[]{:S(2)}) async-start(), calls=%async_computation.4 | async-start | bytes 12779520 | tf_op jit(solution)/shard_map/all_gather | solution.py:120
  7.3 8.7 %copy-start.9 = (s32[128]{0:T(128)S(1)}, s32[128]{0:T(128)}, u32[]{:S(2)}) copy-start(s32[128]{0:T(128)} %param.9) | copy-start | bytes 1540
  16.0 8.9 %copy-start.4 = (bf16[128,2048]{1,0:T(8,128)(2,1)S(1)}, bf16[128,2048]{1,0:T(8,128)(2,1)}, u32[]{:S(2)}) copy-start(bf16[128,2048]{1,0:T(8,128)(2,1)} %param.11) | copy-start | bytes 1572868
  21.0 18.0 %copy-start.5 = (f32[3,3,2048]{2,1,0:T(4,128)S(1)}, f32[3,3,2048]{2,1,0:T(4,128)}, u32[]{:S(2)}) copy-start(f32[3,3,2048]{2,1,0:T(4,128)} %param.13) | copy-start | bytes 221188
  21.1 19.2 %collective-permute-start = (bf16[2,3,2048]{2,1,0:T(4,128)(2,1)S(1)}, bf16[2,3,2048]{2,1,0:T(4,128)(2,1)S(1)}, u32[]{:S(2)}, u32[]{:S(2)}) collective-permute-start(bf16[2,3,2048]{2,1,0:T(4,128)(2,1)S(1)} %slice.111), channel_id=1, source_target_pairs={{0,4},{4,8},{8,12},{12,16},{16,20},{20,24},{24,28},{28,32},{32,36}... | collective-permute-start | bytes 73736 | tf_op jit(solution)/shard_map/ppermute | solution.py:13
  26.5 33.3 %all-to-all-start.1 = ((bf16[128,2,1024]{0,1,2:T(2,128)(2,1)}), bf16[128,2,1024]{0,1,2:T(2,128)(2,1)}, u32[]{:S(2)}, u32[]{:S(2)}) async-start(bf16[128,2,1024]{0,1,2:T(2,128)(2,1)} %copy.104), calls=%async_computation.1 | async-start | bytes 1048576 | tf_op jit(solution)/shard_map/all_to_all | solution.py:110
  59.8 29.0 %all-to-all-start = ((bf16[128,2,1024]{0,1,2:T(2,128)(2,1)}), bf16[128,2,1024]{0,1,2:T(2,128)(2,1)}, u32[]{:S(2)}, u32[]{:S(2)}) async-start(bf16[128,2,1024]{0,1,2:T(2,128)(2,1)} %copy.96), calls=%async_computation | async-start | bytes 1048576 | tf_op jit(solution)/shard_map/all_to_all | solution.py:109
  68.4 323.5 %reduce-scatter.2.cloned.1.call-start = ((), (), s32[]{:S(2)}) async-start(), calls=%async_computation.5 | async-start | bytes 1966080 | tf_op jit(solution)/shard_map/reduce_scatter | solution.py:123
  75.8 2.3 copy-start.3
  93.8 2.7 copy-start
  100.7 1.6 copy-start.1
  100.7 2.2 copy-start.2
  195.6 0.8 copy-start.7
  197.7 139.4 %copy-start.6 = (f32[3,3,256]{2,1,0:T(4,128)S(1)}, f32[3,3,256]{2,1,0:T(4,128)}, u32[]{:S(2)}) copy-start(f32[3,3,256]{2,1,0:T(4,128)} %param.15) | copy-start | bytes 27652
  337.0 59.4 %copy-start.8 = (f32[7,256]{1,0:T(8,128)S(1)}, f32[7,256]{1,0:T(8,128)}, u32[]{:S(2)}) copy-start(f32[7,256]{1,0:T(8,128)} %param.16) | copy-start | bytes 21508
  337.1 73.2 %copy-start.10 = (f32[256]{0:T(256)S(1)}, f32[256]{0:T(256)}, u32[]{:S(2)}) copy-start(f32[256]{0:T(256)} %param.17) | copy-start | bytes 3076
  393.0 8.5 %collective-permute-start.1 = (bf16[2,3,256]{2,0,1:T(2,128)(2,1)S(1)}, bf16[2,3,256]{2,0,1:T(2,128)(2,1)S(1)}, u32[]{:S(2)}, u32[]{:S(2)}) collective-permute-start(bf16[2,3,256]{2,0,1:T(2,128)(2,1)S(1)} %slice.151), channel_id=1, source_target_pairs={{0,4},{4,8},{8,12},{12,16},{16,20},{20,24},{24,28},{28,32},{32,36}... | collective-permute-start | bytes 9224 | tf_op jit(solution)/shard_map/ppermute | solution.py:13
  401.7 8.6 %collective-permute-start.2 = (f32[6,256]{1,0:T(8,128)S(1)}, f32[6,256]{1,0:T(8,128)S(1)}, u32[]{:S(2)}, u32[]{:S(2)}) collective-permute-start(f32[6,256]{1,0:T(8,128)S(1)} %slice_bitcast_fusion.5), channel_id=1, source_target_pairs={{0,4},{4,8},{8,12},{12,16},{16,20},{20,24},{24,28},{28,32},{32,36}... | collective-permute-start | bytes 18440 | tf_op jit(solution)/shard_map/ppermute | solution.py:13
Sparse Core Ops, SparseCore 0:
  9.1 317.5 all-gather.1
  337.2 54.7 reduce-scatter.1
where the time goes:
time: 426 us; the launch traced here: 418 us
  waiting for transfers between devices  209 us (49%)
  local copies, waits for them, and re-layouts  76.9 us (18%)
  matrix products  46.7 us (11%)
  blocking collectives  30.8 us (7%)
  starting transfers between devices  30.5 us (7%)
  between operations  14 us (3%)
  other arithmetic  10.5 us (2%)
    all_gather x1, waiting for transfers between devices, per_device(): lax.all_gather(projection, 'ctx', axis=2, tiled=True)  129 us
    reduce_scatter x1, waiting for transfers between devices, per_device(): lax.psum_scatter(partial_sums, 'ch', scatter_dimension=2, tiled=True)  54.9 us
    unnamed x27, local copies, waits for them, and re-layouts  37 us
    all_to_all x1, blocking collectives, per_device(): lax.all_to_all(convolve(moved), 'ctx', split_axis=0, concat_axis=2, tiled...  30.8 us
    convert_element_type x3, local copies, waits for them, and re-layouts, convolve(): return result.astype(jnp.bfloat16)  13.7 us
    all_to_all x1, starting transfers between devices, per_device(): lax.all_to_all(grouped[1], 'ctx', split_axis=2, concat_axis=0, tiled=True)  12.5 us
    ppermute x3, waiting for transfers between devices, from_behind(): lax.ppermute(value, axis, [(source, source + steps) for source in range(i...  11.6 us
    all_to_all x1, waiting for transfers between devices, per_device(): lax.all_to_all(grouped[1], 'ctx', split_axis=2, concat_axis=0, tiled=True)  11.4 us
  transfers between devices with their start and end apart: 7, of which 6 were waited for; matrix products, arithmetic and copies ran while one was open for 29% of the time, Pallas kernels for 0%

commit v1 on v0

v1 whole, which is shorter than its diff:
```python
import functools

import jax
import jax.numpy as jnp
import numpy as np
from jax import lax
from jax.experimental import pallas as pl
from jax.experimental.pallas import tpu as pltpu
from jax.sharding import PartitionSpec as P

MESH = pl.DeviceIdType.MESH
F32, BF16 = jnp.float32, jnp.bfloat16
NEAR = (0, 1, 7, 2, 6, 3, 5, 4)
SPOT = tuple(NEAR.index(k) for k in range(8))


def dft_tables():
    k1 = np.arange(64)[:, None] + 0.25
    phase = 2 * np.pi * k1 * np.arange(64)[None, :] / 64
    rows = np.concatenate([np.cos(phase), -np.sin(phase)], 0)

    def split(table):
        high = table.astype(BF16)
        return high, (table - high.astype(np.float64)).astype(BF16)

    high, low = split(rows)
    first = np.concatenate([high, low], 1)
    back_high, back_low = high.T, low.T
    last = np.concatenate([back_high, back_high, back_low], 1)
    turn = 2 * np.pi * k1 * np.arange(128)[None, :] / 8192
    inner = 2 * np.pi * np.outer(np.arange(128), np.arange(128)) / 128
    cos, sin = np.cos(inner), np.sin(inner)
    both = np.concatenate([np.concatenate([cos, -sin], 1), np.concatenate([sin, cos], 1)], 0)
    w_high, w_low = split(both)
    return (first, last, w_high, w_low, np.cos(turn).astype(np.float32), np.sin(turn).astype(np.float32))


def dot(left, right):
    return jnp.dot(left, right, preferred_element_type=F32)


def dot_t(left, right):
    return lax.dot_general(left, right, (((1,), (1,)), ((), ())), preferred_element_type=F32)


def halves(value):
    high = value.astype(BF16)
    return high, (value - high.astype(F32)).astype(BF16)


def kernel(
    tok_ref, tab_ref, filt_ref, tin_ref, proj_ref, tout_ref,
    first_ref, last_ref, wh_ref, wl_ref, cos_ref, sin_ref,
    out_ref,
    tok_all, tab_buf, tab_t, tin_t, filt_t, filt_z, filt_x, filt_f, gated, query, long_f,
    spec, send_a, all_a, b_half, b_all, c_send, c_recv, c_mine, y_send, y_recv,
    taps_mine, halo_send, halo_recv, out_send, out_recv,
    tab_sem, tz_s, tz_r, tx_s, tx_r, fz_s, fz_r, fx_s, fx_r, sw_s, sw_r, bp_s, bm_s, b_r,
    az_s, az_r, ax_s, ax_r, cc_s, cc_r, cy_s, cy_r, tp_s, tp_r, h_s, h_r, o_s, o_r,
):
    ctx, ch = lax.axis_index("ctx"), lax.axis_index("ch")
    x, yl, z = ctx // 16, (ctx // 8) % 2, ctx % 8
    yh, core = ch // 2, ch % 2
    xy = x * 2 + yl
    y = yh * 2 + yl

    def dev(x_, yl_, z_, ch_):
        return {"ctx": x_ * 16 + yl_ * 8 + z_, "ch": ch_}

    def z_peer(k):
        return dev(x, yl, lax.rem(z + k, 8), ch)

    def xy_peer(k):
        other = lax.rem(xy + k, 8)
        return dev(other // 2, other % 2, z, ch)

    def x_peer(k):
        return dev(lax.rem(x + k, 4), yl, z, ch)

    core_peer = dev(x, yl, z, yh * 2 + 1 - core)

    def y_peer(k):
        other = lax.rem(y + k, 4)
        return dev(x, other % 2, z, (other // 2) * 2 + core)

    turned = dev(ch, yl, z, x)
    is_turned = x != ch
    place = ch * 16 + yl * 8 + z

    def owner(index):
        return dev(x, (index // 8) % 2, index % 8, index // 16)

    has_next, has_prev = place < 63, place > 0

    def remote(src, dst, send, recv, device):
        return pltpu.make_async_remote_copy(
            src_ref=src, dst_ref=dst, send_sem=send, recv_sem=recv, device_id=device, device_id_type=MESH
        )

    bar = pltpu.get_barrier_semaphore()

    def greet(device):
        pl.semaphore_signal(bar, inc=1, device_id=device, device_id_type=MESH)

    for k in range(1, 8):
        greet(z_peer(k))
        greet(xy_peer(k))
    greet(dev(x, yl, z, (1 - yh) * 2 + core))
    greet(dev(x, 1 - yl, z, (1 - yh) * 2 + core))
    greet(core_peer)
    pl.when(is_turned)(lambda: greet(turned))
    pl.when((z == 7) & has_next)(lambda: greet(owner(place + 1)))
    pl.when((z == 0) & has_prev)(lambda: greet(owner(place - 1)))

    lanes = pl.multiple_of((ctx // 4) * 128, 128)
    tab_copy = pltpu.make_async_copy(tab_ref.at[:, :, pl.ds(lanes, 128)], tab_buf, tab_sem)
    tab_copy.start()
    for group in range(16):
        block = filt_ref[:, group * 128 : (group + 1) * 128].T
        for part in range(4):
            index = group * 4 + part
            filt_t[index // 8, index % 8] = block[part * 32 : (part + 1) * 32]
    for half in range(2):
        for part in range(4):
            start = part * 512 + half * 256
            b_half[half, :, :, part * 256 : (part + 1) * 256] = proj_ref[:, :, start : start + 256]
    tok_all[ctx] = tok_ref[...]
    tin_t[...] = tin_ref[:, pl.ds(lanes, 128)].T
    rows = pl.multiple_of((ctx % 4) * 32, 32)
    tin = tin_t[pl.ds(rows, 32), :]

    expected = 17 + jnp.where(is_turned, 1, 0)
    expected += jnp.where((z == 7) & has_next, 1, 0) + jnp.where((z == 0) & has_prev, 1, 0)
    pl.semaphore_wait(bar, expected)

    def tok_z(k):
        return remote(tok_all.at[ctx], tok_all.at[ctx], tz_s.at[k], tz_r.at[k], z_peer(k))

    def filt_along_z(k):
        return remote(
            filt_t.at[:, lax.rem(z + k, 8)], filt_z.at[:, SPOT[k]], fz_s.at[k], fz_r.at[k], z_peer(k)
        )

    for k in range(1, 8):
        tok_z(k).start()
    for k in NEAR[1:]:
        filt_along_z(k).start()
    swap = remote(b_half.at[1 - yl], b_all.at[:, yl, z], sw_s, sw_r, dev(x, 1 - yl, z, ch))
    swap.start()
    taps_copy = remote(tout_ref, taps_mine, tp_s, tp_r, turned)
    pl.when(is_turned)(lambda: taps_copy.start())

    @pl.when(x == ch)
    def _():
        taps_mine[...] = tout_ref[...]

    b_all[:, yl, z] = b_half[yl]
    for other in range(8):
        filt_z[other, 0] = filt_t[other, z]
    tab_copy.wait()
    for j in range(3):
        tab_t[...] = tab_buf[j].T
        spec[pl.ds(32 * j, 32), 0:512] = tab_t[pl.ds(rows, 32), :].astype(F32)
    table = spec[0:96, 0:512].astype(BF16)

    def tok_x(k):
        line = tok_all.at[pl.ds(xy * 8, 8)]
        return remote(line, line, tx_s.at[k], tx_r.at[k], xy_peer(k))

    for k in range(1, 8):
        tok_z(k).wait()
    for k in range(1, 8):
        tok_x(k).start()

    def filt_over_x(wave, k):
        spots = pl.ds(0, 5) if wave == 0 else pl.ds(5, 3)
        other = lax.rem(xy + k, 8)
        return remote(
            filt_z.at[other, spots], filt_x.at[xy, spots], fx_s.at[wave, k], fx_r.at[wave, k], xy_peer(k)
        )

    for k in range(1, 8):
        tok_x(k).wait()

    def embed(chunk, carry):
        ids = jnp.concatenate([tok_all[chunk * 4 + i] for i in range(4)], 1)
        hot = (lax.broadcasted_iota(jnp.int32, (512, 512), 0) == ids).astype(F32).astype(BF16)
        value = dot(table, hot)
        wide = jnp.concatenate([carry, value], 1)
        total = None
        parts = []
        for j in range(3):
            total = tin[:, j : j + 1] * value[32 * j : 32 * j + 32]
            for s in (1, 2):
                moved = pltpu.roll(wide[32 * j : 32 * j + 32], s, 1)[:, 128:]
                total = total + tin[:, 3 * s + j : 3 * s + j + 1] * moved
            parts.append(total)
        gate = (parts[1] * parts[2]).astype(BF16).astype(F32)
        for i in range(4):
            at = pl.ds(pl.multiple_of((chunk * 4 + i) * 32, 32), 32)
            gated[at, :] = gate[:, i * 128 : (i + 1) * 128]
            query[at, :] = parts[0][:, i * 128 : (i + 1) * 128]
        return value[:, 384:]

    carry = lax.fori_loop(0, 8, embed, jnp.zeros((96, 128), F32))
    for k in NEAR[1:5]:
        filt_along_z(k).wait()
    for k in range(1, 8):
        filt_over_x(0, k).start()
    carry = lax.fori_loop(8, 16, embed, carry)
    for k in NEAR[5:]:
        filt_along_z(k).wait()
    for k in range(1, 8):
        filt_over_x(1, k).start()
    filt_x[xy] = filt_z[xy]

    def ring(direction, step):
        which = lax.rem(z + (8 - step if direction > 0 else step), 8)
        chunk = b_all.at[:, :, which]
        sems = (bp_s if direction > 0 else bm_s).at[step]
        return remote(chunk, chunk, sems, b_r.at[direction, step], z_peer(1 if direction > 0 else 7))

    swap.wait()
    ring(1, 0).start()
    ring(0, 0).start()

    def forward(source, group):
        columns = [source[pl.ds(group * 4 + i, 64, stride=32), :] for i in range(4)]
        column = jnp.concatenate(columns, 1).astype(BF16)
        stage = dot(first_ref[...], jnp.concatenate([column, column], 0))
        cos, sin = cos_ref[...], sin_ref[...]
        turned_rows = []
        for i in range(4):
            re, im = stage[:64, i * 128 : (i + 1) * 128], stage[64:, i * 128 : (i + 1) * 128]
            turned_rows.append(jnp.concatenate([re * cos + im * sin, im * cos - re * sin], 1))
        high, low = halves(jnp.concatenate(turned_rows, 0))
        return dot(high, wh_ref[...]) + (dot(low, wh_ref[...]) + dot(high, wl_ref[...]))

    def signal_side(group, _):
        spec[pl.ds(pl.multiple_of(group * 256, 256), 256), 0:256] = forward(gated, group)
        return 0

    lax.fori_loop(0, 8, signal_side, 0)
    for wave in range(2):
        for k in range(1, 8):
            filt_over_x(wave, k).wait()
    for step in range(3):
        ring(1, step).wait()
        ring(1, step + 1).start()
        ring(0, step).wait()
        if step < 2:
            ring(0, step + 1).start()
    for other in range(8):
        for spot in range(8):
            from_z = lax.rem(z + 8 - NEAR[spot], 8)
            at = pl.ds(pl.multiple_of((other * 8 + from_z) * 32, 32), 32)
            filt_f[at, :] = filt_x[other, spot].astype(F32)

    def filter_side(group, _):
        h = forward(filt_f, group)
        s = spec[pl.ds(pl.multiple_of(group * 256, 256), 256), 0:256]
        sr, si, hr, hi = s[:, :128], s[:, 128:], h[:, :128], h[:, 128:]
        high, low = halves(jnp.concatenate([sr * hr - si * hi, sr * hi + si * hr], 1))
        back = dot_t(high, wh_ref[...]) + (dot_t(low, wh_ref[...]) + dot_t(high, wl_ref[...]))
        cos, sin = cos_ref[...], sin_ref[...]
        parts = []
        for i in range(4):
            re, im = back[i * 64 : (i + 1) * 64, :128], back[i * 64 : (i + 1) * 64, 128:]
            parts.append(jnp.concatenate([re * cos - im * sin, im * cos + re * sin], 0))
        high, low = halves(jnp.concatenate(parts, 1))
        result = dot(last_ref[...], jnp.concatenate([high, low, high], 0)) * (1.0 / 8192)
        for i in range(4):
            long_f[pl.ds(group * 4 + i, 64, stride=32), :] = result[:, i * 128 : (i + 1) * 128]
        return 0

    lax.fori_loop(0, 8, filter_side, 0)

    skip = jnp.broadcast_to(tin[:, 9:10], (32, 128))
    for index in range(64):
        x_, yl_, z_ = index // 16, (index // 8) % 2, index % 8
        at = pl.ds(index * 32, 32)
        rounded = long_f[at, :].astype(BF16).astype(F32)
        value = (query[at, :] * (rounded + skip * gated[at, :])).astype(BF16)
        send_a[(x_ // 2) * 2 + yl_, x_ % 2, z_] = value

    order = [lax.rem(y + off, 4) for off in (2, 1, 3, 0)]

    def a_z(t, k):
        q = order[t]
        return remote(
            send_a.at[q, :, lax.rem(z + k, 8)], all_a.at[x, q, :, z], az_s.at[t, k], az_r.at[t, k], z_peer(k)
        )

    def a_x(t, k):
        mine = all_a.at[x, order[t]]
        return remote(mine, mine, ax_s.at[t, k], ax_r.at[t, k], x_peer(k))

    for t in range(4):
        for k in NEAR[1:]:
            a_z(t, k).start()
        all_a[x, order[t], :, z] = send_a[order[t], :, z]
    ring(1, 3).wait()

    def c_core(t):
        return remote(c_send.at[t], c_recv.at[t], cc_s.at[t], cc_r.at[t], core_peer)

    def c_y(t):
        return remote(y_send.at[t], y_recv.at[t], cy_s.at[t], cy_r.at[t], y_peer((2, 1, 3)[t]))

    def after_core(t):
        c_core(t).wait()
        total = c_mine[t] + c_recv[t].astype(F32)
        if t < 3:
            y_send[t] = total.astype(BF16)
            c_y(t).start()
        else:
            c_mine[t] = total

    for t in range(4):
        for k in NEAR[1:]:
            a_z(t, k).wait()
        for k in range(1, 4):
            a_x(t, k).start()
    for t in range(4):
        for k in range(1, 4):
            a_x(t, k).wait()

        def columns(part, _):
            at = pl.ds(pl.multiple_of(part * 256, 256), 256)
            total = None
            for xs in range(4):
                blocks = [all_a[xs, order[t], lo].reshape(256, 128) for lo in range(2)]
                weights = b_all[part].reshape(256, 1024)[:, xs * 256 : (xs + 1) * 256]
                term = dot(weights, jnp.concatenate(blocks, 1))
                total = term if total is None else total + term
            @pl.when(core == 0)
            def _():
                c_mine[t, at, :] = total[:, :128]
                c_send[t, at, :] = total[:, 128:].astype(BF16)

            @pl.when(core == 1)
            def _():
                c_mine[t, at, :] = total[:, 128:]
                c_send[t, at, :] = total[:, :128].astype(BF16)

            return 0

        lax.fori_loop(0, 3, columns, 0)
        c_core(t).start()
        if t > 0:
            after_core(t - 1)
    after_core(3)
    for t in range(3):
        c_y(t).wait()
    summed = c_mine[3] + y_recv[0].astype(F32) + y_recv[1].astype(F32) + y_recv[2].astype(F32)
    projected = jnp.concatenate([summed[i * 128 : (i + 1) * 128].T for i in range(6)], 1).astype(BF16)

    halo = remote(halo_send, halo_recv, h_s, h_r, owner(place + 1))
    halo_send[...] = projected[112:]
    pl.when(has_next)(lambda: halo.start())

    @pl.when(place == 0)
    def _():
        halo_recv[...] = jnp.zeros_like(halo_recv)

    pl.when(has_next)(lambda: halo.wait_send())
    pl.when(has_prev)(lambda: halo.wait_recv())
    pl.when(is_turned)(lambda: taps_copy.wait())
    wide = jnp.concatenate([halo_recv[...], projected], 0).astype(F32)

    def shifted(value, s):
        return value if s == 0 else pltpu.roll(value, s, 0)

    feats = []
    for j in range(3):
        part = wide[:, j * 256 : (j + 1) * 256]
        total = None
        for s in range(3):
            term = taps_mine[3 * s + j : 3 * s + j + 1, :] * shifted(part, s)
            total = term if total is None else total + term
        feats.append(total)
    gate = feats[1] * feats[2]
    short = None
    for s in range(7):
        term = taps_mine[9 + s : 10 + s, :] * shifted(gate, s)
        short = term if short is None else short + term
    mixed = (feats[0] * (short + taps_mine[16:17, :] * gate))[16:].astype(BF16)

    out_send[...] = mixed
    out_copy = remote(out_send, out_recv, o_s, o_r, turned)

    @pl.when(is_turned)
    def _():
        out_copy.start()
        out_copy.wait()

    @pl.when(x == ch)
    def _():
        out_recv[...] = out_send[...]

    out_ref[...] = out_recv[...]


def per_device(token_ids, tables, filter_long, skip_long, taps_in, projection, taps_proj, taps_short, skip_short):
    tin = jnp.concatenate([taps_in.reshape(9, 2048), skip_long[None], jnp.zeros((6, 2048), F32)], 0)
    tout = jnp.concatenate(
        [taps_proj.reshape(9, 256), taps_short, skip_short[None], jnp.zeros((7, 256), F32)], 0
    )
    vmem = pl.BlockSpec(memory_space=pltpu.VMEM)
    dma = pltpu.SemaphoreType.DMA
    scratch = [
        pltpu.VMEM((64, 1, 128), jnp.int32),
        pltpu.VMEM((3, 512, 128), BF16),
        pltpu.VMEM((128, 512), BF16),
        pltpu.VMEM((128, 16), F32),
        pltpu.VMEM((8, 8, 32, 128), BF16),
        pltpu.VMEM((8, 8, 32, 128), BF16),
        pltpu.VMEM((8, 8, 32, 128), BF16),
        pltpu.VMEM((2048, 128), F32),
        pltpu.VMEM((2048, 128), F32),
        pltpu.VMEM((2048, 128), F32),
        pltpu.VMEM((2048, 128), F32),
        pltpu.VMEM((2048, 512), F32),
        pltpu.VMEM((4, 2, 8, 32, 128), BF16),
        pltpu.VMEM((4, 4, 2, 8, 32, 128), BF16),
        pltpu.VMEM((2, 3, 16, 1024), BF16),
        pltpu.VMEM((3, 2, 8, 16, 1024), BF16),
        pltpu.VMEM((4, 768, 128), BF16),
        pltpu.VMEM((4, 768, 128), BF16),
        pltpu.VMEM((4, 768, 128), F32),
        pltpu.VMEM((3, 768, 128), BF16),
        pltpu.VMEM((3, 768, 128), BF16),
        pltpu.VMEM((24, 256), F32),
        pltpu.VMEM((16, 768), BF16),
        pltpu.VMEM((16, 768), BF16),
        pltpu.VMEM((128, 256), BF16),
        pltpu.VMEM((128, 256), BF16),
        dma, dma((8,)), dma((8,)), dma((8,)), dma((8,)),
        dma((8,)), dma((8,)), dma((2, 8)), dma((2, 8)),
        dma, dma, dma((4,)), dma((4,)), dma((2, 4)),
        dma((4, 8)), dma((4, 8)), dma((4, 4)), dma((4, 4)),
        dma((4,)), dma((4,)), dma((3,)), dma((3,)),
        dma, dma, dma, dma, dma, dma,
    ]
    return pl.pallas_call(
        kernel,
        out_shape=jax.ShapeDtypeStruct((128, 256), BF16),
        in_specs=[vmem, pl.BlockSpec(memory_space=pl.ANY)] + [vmem] * 10,
        out_specs=vmem,
        scratch_shapes=scratch,
        compiler_params=pltpu.CompilerParams(
            collective_id=0, has_side_effects=True, vmem_limit_bytes=48 * 2**20
        ),
    )(
        token_ids.reshape(1, 128), jnp.transpose(tables, (1, 0, 2)), filter_long, tin,
        jnp.transpose(projection, (1, 2, 0)), tout, *[jnp.asarray(t) for t in dft_tables()],
    )


def solution(mesh):
    placed = (
        P("ctx"),
        P(None, None, "ch"),
        P("ctx", "ch"),
        P("ch"),
        P(None, None, "ch"),
        P("ch", None, "ctx"),
        P(None, None, "ch"),
        P(None, "ch"),
        P("ch"),
    )
    return jax.shard_map(
        per_device, mesh=mesh, in_specs=placed, out_specs=P("ctx", "ch"), check_vma=False
    )
```

time: 426 us -> 107 us (0.25); the launches traced: 418 us -> 106 us
  waiting for transfers between devices: 209 us -> 0 us
  Pallas kernels: 0 us -> 94.5 us
  local copies, waits for them, and re-layouts: 76.9 us -> 9.94 us
  matrix products: 46.7 us -> 0 us
  blocking collectives: 30.8 us -> 0 us
  starting transfers between devices: 30.5 us -> 0 us
  between operations: 14 us -> 0.04 us
  other arithmetic: 10.5 us -> 1.56 us
    all_gather x1 -> x0, waiting for transfers between devices: 129 us -> none  [per_device(): lax.all_gather(projection, 'ctx', axis=2, tiled=True)]
    pallas_call x0 -> x1, Pallas kernels: none -> 94.5 us  [per_device(): pl.pallas_call(kernel, out_shape=jax.ShapeDtypeStruct((128, 256), BF16),...]
    reduce_scatter x1 -> x0, waiting for transfers between devices: 54.9 us -> none  [per_device(): lax.psum_scatter(partial_sums, 'ch', scatter_dimension=2, tiled=True)]
    dot_general x18 -> x0, matrix products: 43.2 us -> none  [the longest x1 10.3 us: per_device(): jnp.einsum('te,ejc->tjc', layer_one, lax.all_gather(projection, 'ctx', ax...]
    all_to_all x1 -> x0, blocking collectives: 30.8 us -> none  [per_device(): lax.all_to_all(convolve(moved), 'ctx', split_axis=0, concat_axis=2, tiled...]
    unnamed x27 -> x19, local copies, waits for them, and re-layouts: 37 us -> 8.13 us
    all_to_all x2 -> x0, starting transfers between devices: 21.1 us -> none  [the longest x1 12.5 us: per_device(): lax.all_to_all(grouped[1], 'ctx', split_axis=2, concat_axis=0, tiled=True)]
    convert_element_type x6 -> x0, local copies, waits for them, and re-layouts: 16.6 us -> none  [the longest x3 13.7 us: convolve(): return result.astype(jnp.bfloat16)]
  transfers between devices with their start and end apart: 7 -> 0, of which waited for: 6 -> 0; matrix products, arithmetic and copies ran while one was open for 29% -> 0% of each run, Pallas kernels for 0% -> 0%
where the time goes in v1:
time: 107 us; the launch traced here: 106 us
  Pallas kernels  94.5 us (88%)
  local copies, waits for them, and re-layouts  9.94 us (9%)
  other arithmetic  1.56 us (1%)
    pallas_call x1, Pallas kernels, per_device(): pl.pallas_call(kernel, out_shape=jax.ShapeDtypeStruct((128, 256), BF16),...  94.5 us
    unnamed x19, local copies, waits for them, and re-layouts  8.13 us

profile of v1, /device:TPU:6, one launch (start us, length us, event | category | flops | bytes accessed | tf_op | source)
XLA Modules:
  0.0 106.0 jit_solution(9828445638953003257)
XLA Ops:
  0.0 0.9 reshape.10
  0.9 0.1 pad.6.clone
  1.0 0.8 maximum_maximum_fusion.tin_ref
  1.8 0.7 reshape.11
  2.5 0.1 pad.3.clone
  2.6 0.8 maximum_maximum_fusion.1.tout_ref
  3.4 0.0 copy-start
  3.4 1.0 copy-done
  4.4 0.0 copy-start.1
  4.4 0.9 copy-done.1
  5.3 0.0 copy-start.2
  5.4 0.9 copy-done.2
  6.3 0.0 copy-start.3
  6.3 0.9 copy-done.3
  7.2 0.0 copy-start.4
  7.2 0.8 copy-done.4
  8.0 0.0 copy-start.5
  8.0 0.8 copy-done.5
  8.7 0.0 copy-start.6
  8.7 0.8 copy-done.6
  9.5 0.8 copy-done.7
  10.2 0.7 copy-done.8
  10.9 94.5 %shard_map.145 = bf16[128,256]{1,0:T(8,128)(2,1)S(1)} custom-call(s32[1,128]{1,0:T(1,128)S(1)} %bitcast.6, bf16[3,512,2048]{2,1,0:T(8,128)(2,1)} %bitcast.7, bf16[128,2048]{1,0:T(8,128)(2,1)S(1)} %copy-done, f32[16,2048]{1,0:T(8,128)S(1)} %maximum_maximum_fusion.tin_ref, bf16[3,16,2048]{2,1,0:T(8,128)(2,1)S(1)} %bitcast.5, ...), custom_call_target="tpu_custom_call" | custom-call | tf_op jit(solution)/shard_map/pallas_call | solution.py:445
  105.4 0.6 copy.17
  (4 shorter events, 0.0 us)
Async XLA Ops:
  3.4 1.0 copy-start
  4.4 0.9 copy-start.1
  5.3 0.9 copy-start.2
  6.3 0.9 copy-start.3
  7.2 0.8 copy-start.4
  8.0 0.8 copy-start.5
  8.7 0.8 copy-start.6
  9.5 0.8 copy-start.7
  10.2 0.7 copy-start.8

commit v2 on v1

--- a/solution.py
+++ b/solution.py
@@ -32,7 +32,8 @@
     cos, sin = np.cos(inner), np.sin(inner)
     both = np.concatenate([np.concatenate([cos, -sin], 1), np.concatenate([sin, cos], 1)], 0)
     w_high, w_low = split(both)
-    return (first, last, w_high, w_low, np.cos(turn).astype(np.float32), np.sin(turn).astype(np.float32))
+    tall = [first, *np.split(last, 3, 1), *np.split(w_high, 2, 1), *np.split(w_low, 2, 1)]
+    return np.concatenate(tall, 0), np.concatenate([np.cos(turn), np.sin(turn)], 0).astype(np.float32)
 
 
 def dot(left, right):
@@ -49,9 +50,11 @@
 
 
 def kernel(
-    tok_ref, tab_ref, filt_ref, tin_ref, proj_ref, tout_ref,
-    first_ref, last_ref, wh_ref, wl_ref, cos_ref, sin_ref,
+    tok_hbm, tab_hbm, filt_hbm, tin_hbm, skip_hbm, proj_hbm, tpr_hbm, tsh_hbm, ssk_hbm,
+    dft_hbm, turn_hbm,
     out_ref,
+    tok_ref, filt_ref, tin_ref, skip_ref, proj_ref, tpr_ref, tsh_ref, ssk_ref,
+    dft_ref, turn_ref, tout_ref, load_sem,
     tok_all, tab_buf, tab_t, tin_t, filt_t, filt_z, filt_x, filt_f, gated, query, long_f,
     spec, send_a, all_a, b_half, b_all, c_send, c_recv, c_mine, y_send, y_recv,
     taps_mine, halo_send, halo_recv, out_send, out_recv,
@@ -97,6 +100,18 @@
             src_ref=src, dst_ref=dst, send_sem=send, recv_sem=recv, device_id=device, device_id_type=MESH
         )
 
+    lanes = pl.multiple_of((ctx // 4) * 128, 128)
+    tab_copy = pltpu.make_async_copy(tab_hbm.at[:, :, pl.ds(lanes, 128)], tab_buf, tab_sem)
+    pairs = (
+        (filt_hbm, filt_ref), (tok_hbm, tok_ref), (proj_hbm, proj_ref), (tin_hbm, tin_ref),
+        (skip_hbm, skip_ref), (tpr_hbm, tpr_ref), (tsh_hbm, tsh_ref), (ssk_hbm, ssk_ref),
+        (dft_hbm, dft_ref), (turn_hbm, turn_ref),
+    )
+    loads = [pltpu.make_async_copy(src, dst, load_sem.at[i]) for i, (src, dst) in enumerate(pairs)]
+    for load in loads:
+        load.start()
+    tab_copy.start()
+
     bar = pltpu.get_barrier_semaphore()
 
     def greet(device):
@@ -112,20 +127,26 @@
     pl.when((z == 7) & has_next)(lambda: greet(owner(place + 1)))
     pl.when((z == 0) & has_prev)(lambda: greet(owner(place - 1)))
 
-    lanes = pl.multiple_of((ctx // 4) * 128, 128)
-    tab_copy = pltpu.make_async_copy(tab_ref.at[:, :, pl.ds(lanes, 128)], tab_buf, tab_sem)
-    tab_copy.start()
+    loads[0].wait()
     for group in range(16):
         block = filt_ref[:, group * 128 : (group + 1) * 128].T
         for part in range(4):
             index = group * 4 + part
             filt_t[index // 8, index % 8] = block[part * 32 : (part + 1) * 32]
+    for load in loads[1:]:
+        load.wait()
     for half in range(2):
         for part in range(4):
             start = part * 512 + half * 256
             b_half[half, :, :, part * 256 : (part + 1) * 256] = proj_ref[:, :, start : start + 256]
     tok_all[ctx] = tok_ref[...]
-    tin_t[...] = tin_ref[:, pl.ds(lanes, 128)].T
+    stacked = [tin_ref[s, :, pl.ds(lanes, 128)] for s in range(3)] + [skip_ref[pl.ds(ctx // 4, 1), :]]
+    tin_t[...] = jnp.concatenate(stacked + [jnp.zeros((6, 128), F32)], 0).T
+    for s in range(3):
+        tout_ref[3 * s : 3 * s + 3, :] = tpr_ref[s]
+    tout_ref[9:16, :] = tsh_ref[...]
+    tout_ref[16:17, :] = jnp.concatenate([ssk_ref[0:1, :], ssk_ref[1:2, :]], 1)
+    tout_ref[17:24, :] = jnp.zeros((7, 256), F32)
     rows = pl.multiple_of((ctx % 4) * 32, 32)
     tin = tin_t[pl.ds(rows, 32), :]
 
@@ -216,40 +237,57 @@
 
     def ring(direction, step):
         which = lax.rem(z + (8 - step if direction > 0 else step), 8)
-        chunk = b_all.at[:, :, which]
+        chunk = b_all.at[:, :, which] if step < 3 else b_all.at[:, 0 if direction > 0 else 1, which]
         sems = (bp_s if direction > 0 else bm_s).at[step]
         return remote(chunk, chunk, sems, b_r.at[direction, step], z_peer(1 if direction > 0 else 7))
+
+    def ring_on(step):
+        for direction in (1, 0):
+            ring(direction, step).wait()
+            if step < 3:
+                ring(direction, step + 1).start()
 
     swap.wait()
     ring(1, 0).start()
     ring(0, 0).start()
 
+    def first():
+        return dft_ref[0:128, :]
+
+    def last():
+        return jnp.concatenate([dft_ref[128 + 64 * i : 192 + 64 * i, :] for i in range(3)], 1)
+
+    def w_high():
+        return jnp.concatenate([dft_ref[320:576, :], dft_ref[576:832, :]], 1)
+
+    def w_low():
+        return jnp.concatenate([dft_ref[832:1088, :], dft_ref[1088:1344, :]], 1)
+
+    def turns():
+        return turn_ref[0:64, :], turn_ref[64:128, :]
+
     def forward(source, group):
         columns = [source[pl.ds(group * 4 + i, 64, stride=32), :] for i in range(4)]
         column = jnp.concatenate(columns, 1).astype(BF16)
-        stage = dot(first_ref[...], jnp.concatenate([column, column], 0))
-        cos, sin = cos_ref[...], sin_ref[...]
+        stage = dot(first(), jnp.concatenate([column, column], 0))
+        cos, sin = turns()
         turned_rows = []
         for i in range(4):
             re, im = stage[:64, i * 128 : (i + 1) * 128], stage[64:, i * 128 : (i + 1) * 128]
             turned_rows.append(jnp.concatenate([re * cos + im * sin, im * cos - re * sin], 1))
         high, low = halves(jnp.concatenate(turned_rows, 0))
-        return dot(high, wh_ref[...]) + (dot(low, wh_ref[...]) + dot(high, wl_ref[...]))
+        return dot(high, w_high()) + (dot(low, w_high()) + dot(high, w_low()))
 
     def signal_side(group, _):
         spec[pl.ds(pl.multiple_of(group * 256, 256), 256), 0:256] = forward(gated, group)
         return 0
 
     lax.fori_loop(0, 8, signal_side, 0)
-    for wave in range(2):
-        for k in range(1, 8):
-            filt_over_x(wave, k).wait()
-    for step in range(3):
-        ring(1, step).wait()
-        ring(1, step + 1).start()
-        ring(0, step).wait()
-        if step < 2:
-            ring(0, step + 1).start()
+    for k in range(1, 8):
+        filt_over_x(0, k).wait()
+    ring_on(0)
+    for k in range(1, 8):
+        filt_over_x(1, k).wait()
     for other in range(8):
         for spot in range(8):
             from_z = lax.rem(z + 8 - NEAR[spot], 8)
@@ -261,14 +299,14 @@
         s = spec[pl.ds(pl.multiple_of(group * 256, 256), 256), 0:256]
         sr, si, hr, hi = s[:, :128], s[:, 128:], h[:, :128], h[:, 128:]
         high, low = halves(jnp.concatenate([sr * hr - si * hi, sr * hi + si * hr], 1))
-        back = dot_t(high, wh_ref[...]) + (dot_t(low, wh_ref[...]) + dot_t(high, wl_ref[...]))
-        cos, sin = cos_ref[...], sin_ref[...]
+        back = dot_t(high, w_high()) + (dot_t(low, w_high()) + dot_t(high, w_low()))
+        cos, sin = turns()
         parts = []
         for i in range(4):
             re, im = back[i * 64 : (i + 1) * 64, :128], back[i * 64 : (i + 1) * 64, 128:]
             parts.append(jnp.concatenate([re * cos - im * sin, im * cos + re * sin], 0))
         high, low = halves(jnp.concatenate(parts, 1))
-        result = dot(last_ref[...], jnp.concatenate([high, low, high], 0)) * (1.0 / 8192)
+        result = dot(last(), jnp.concatenate([high, low, high], 0)) * (1.0 / 8192)
         for i in range(4):
             long_f[pl.ds(group * 4 + i, 64, stride=32), :] = result[:, i * 128 : (i + 1) * 128]
         return 0
@@ -291,15 +329,24 @@
             send_a.at[q, :, lax.rem(z + k, 8)], all_a.at[x, q, :, z], az_s.at[t, k], az_r.at[t, k], z_peer(k)
         )
 
-    def a_x(t, k):
+    def a_x(t, right):
         mine = all_a.at[x, order[t]]
-        return remote(mine, mine, ax_s.at[t, k], ax_r.at[t, k], x_peer(k))
+        return remote(mine, mine, ax_s.at[t, right], ax_r.at[t, right], x_peer(1 if right else 3))
+
+    def a_on(t, right):
+        half = all_a.at[lax.rem(x + (3 if right else 1), 4), order[t], right]
+        return remote(half, half, ax_s.at[t, 2 + right], ax_r.at[t, 2 + right], x_peer(1 if right else 3))
+
+    def pass_on(t):
+        for right in (1, 0):
+            a_x(t, right).wait()
+            a_on(t, right).start()
 
     for t in range(4):
         for k in NEAR[1:]:
             a_z(t, k).start()
         all_a[x, order[t], :, z] = send_a[order[t], :, z]
-    ring(1, 3).wait()
+    ring_on(1)
 
     def c_core(t):
         return remote(c_send.at[t], c_recv.at[t], cc_s.at[t], cc_r.at[t], core_peer)
@@ -319,11 +366,16 @@
     for t in range(4):
         for k in NEAR[1:]:
             a_z(t, k).wait()
-        for k in range(1, 4):
-            a_x(t, k).start()
+        for right in (1, 0):
+            a_x(t, right).start()
+        if t > 0:
+            pass_on(t - 1)
+    ring_on(2)
+    pass_on(3)
+    ring_on(3)
     for t in range(4):
-        for k in range(1, 4):
-            a_x(t, k).wait()
+        for right in (1, 0):
+            a_on(t, right).wait()
 
         def columns(part, _):
             at = pl.ds(pl.multiple_of(part * 256, 256), 256)
@@ -402,13 +454,22 @@
 
 
 def per_device(token_ids, tables, filter_long, skip_long, taps_in, projection, taps_proj, taps_short, skip_short):
-    tin = jnp.concatenate([taps_in.reshape(9, 2048), skip_long[None], jnp.zeros((6, 2048), F32)], 0)
-    tout = jnp.concatenate(
-        [taps_proj.reshape(9, 256), taps_short, skip_short[None], jnp.zeros((7, 256), F32)], 0
-    )
     vmem = pl.BlockSpec(memory_space=pltpu.VMEM)
+    hbm = pl.BlockSpec(memory_space=pltpu.HBM)
+    tables_dft = [jnp.asarray(t) for t in dft_tables()]
     dma = pltpu.SemaphoreType.DMA
     scratch = [
+        pltpu.VMEM((1, 128), jnp.int32),
+        pltpu.VMEM((128, 2048), BF16),
+        pltpu.VMEM((3, 3, 2048), F32),
+        pltpu.VMEM((16, 128), F32),
+        pltpu.VMEM((3, 16, 2048), BF16),
+        pltpu.VMEM((3, 3, 256), F32),
+        pltpu.VMEM((7, 256), F32),
+        pltpu.VMEM((2, 128), F32),
+        *[pltpu.VMEM(t.shape, t.dtype) for t in tables_dft],
+        pltpu.VMEM((24, 256), F32),
+        dma((10,)),
         pltpu.VMEM((64, 1, 128), jnp.int32),
         pltpu.VMEM((3, 512, 128), BF16),
         pltpu.VMEM((128, 512), BF16),
@@ -445,15 +506,16 @@
     return pl.pallas_call(
         kernel,
         out_shape=jax.ShapeDtypeStruct((128, 256), BF16),
-        in_specs=[vmem, pl.BlockSpec(memory_space=pl.ANY)] + [vmem] * 10,
+        in_specs=[hbm] * 11,
         out_specs=vmem,
         scratch_shapes=scratch,
         compiler_params=pltpu.CompilerParams(
-            collective_id=0, has_side_effects=True, vmem_limit_bytes=48 * 2**20
+            collective_id=0, has_side_effects=True, vmem_limit_bytes=60 * 2**20
         ),
     )(
-        token_ids.reshape(1, 128), jnp.transpose(tables, (1, 0, 2)), filter_long, tin,
-        jnp.transpose(projection, (1, 2, 0)), tout, *[jnp.asarray(t) for t in dft_tables()],
+        token_ids.reshape(1, 128), jnp.transpose(tables, (1, 0, 2)), filter_long, taps_in,
+        skip_long.reshape(16, 128), jnp.transpose(projection, (1, 2, 0)), taps_proj, taps_short,
+        skip_short.reshape(2, 128), *tables_dft,
     )
 
 

time: 107 us -> 88.8 us (0.83)
  local copies, waits for them, and re-layouts: 9.94 us -> 1.47 us
  Pallas kernels: 94.5 us -> 86.9 us
  other arithmetic: 1.56 us -> 0 us
    pallas_call x1, Pallas kernels: 94.5 us -> 86.9 us  [per_device(): pl.pallas_call(kernel, out_shape=jax.ShapeDtypeStruct((128, 256), BF16),...]
    unnamed x19 -> x1, local copies, waits for them, and re-layouts: 8.13 us -> 1.47 us
    reshape x2 -> x0, local copies, waits for them, and re-layouts: 1.65 us -> none  [the longest x1 0.93 us: per_device(): taps_in.reshape(9, 2048)]
    concatenate x2 -> x0, other arithmetic: 1.56 us -> none  [the longest x1 0.78 us: per_device(): jnp.concatenate([taps_proj.reshape(9, 256), taps_short, skip_short[None],...]
where the time goes in v2:
time: 88.8 us; the launch traced here: 88.4 us
  Pallas kernels  86.9 us (98%)
  local copies, waits for them, and re-layouts  1.47 us (2%)
    pallas_call x1, Pallas kernels, per_device(): pl.pallas_call(kernel, out_shape=jax.ShapeDtypeStruct((128, 256), BF16),...  86.9 us

profile of v2, /device:TPU:6, one launch (start us, length us, event | category | flops | bytes accessed | tf_op | source)
XLA Modules:
  0.0 88.4 jit_solution(7424545538472220209)
XLA Ops:
  0.0 86.9 %shard_map.109 = bf16[128,256]{1,0:T(8,128)(2,1)} custom-call(s32[1,128]{1,0:T(1,128)} %bitcast.9, bf16[3,512,2048]{2,1,0:T(8,128)(2,1)} %bitcast.5, bf16[128,2048]{1,0:T(8,128)(2,1)} %filt_hbm.1, f32[3,3,2048]{2,1,0:T(4,128)} %tin_hbm.1, f32[16,128]{1,0:T(8,128)} %bitcast.7, bf16[3,16,2048]{2,1,0:T(8,128)(2,1)} %bitcast.6, f32[3,3,256]{2,1,0:T(4,128)} %tpr_hbm.1, ...), custom_call_target="tpu_custom_call" | custom-call | tf_op jit(solution)/shard_map/pallas_call | solution.py:506
  86.9 1.5 %copy.13 = bf16[128,256]{1,0:T(8,128)(2,1)} copy(bf16[128,256]{1,0:T(8,128)(2,1)} %shard_map.109) | data formatting | bytes 131072

commit v3 on v2

--- a/solution.py
+++ b/solution.py
@@ -11,6 +11,7 @@
 MESH = pl.DeviceIdType.MESH
 F32, BF16 = jnp.float32, jnp.bfloat16
 NEAR = (0, 1, 7, 2, 6, 3, 5, 4)
+WAVES = (0, 5, 7, 8)
 SPOT = tuple(NEAR.index(k) for k in range(8))
 
 
@@ -25,14 +26,12 @@
 
     high, low = split(rows)
     first = np.concatenate([high, low], 1)
-    back_high, back_low = high.T, low.T
-    last = np.concatenate([back_high, back_high, back_low], 1)
     turn = 2 * np.pi * k1 * np.arange(128)[None, :] / 8192
     inner = 2 * np.pi * np.outer(np.arange(128), np.arange(128)) / 128
     cos, sin = np.cos(inner), np.sin(inner)
     both = np.concatenate([np.concatenate([cos, -sin], 1), np.concatenate([sin, cos], 1)], 0)
-    w_high, w_low = split(both)
-    tall = [first, *np.split(last, 3, 1), *np.split(w_high, 2, 1), *np.split(w_low, 2, 1)]
+    w_high = both.astype(BF16)
+    tall = [first, high.T, low.T, *np.split(w_high, 2, 1)]
     return np.concatenate(tall, 0), np.concatenate([np.cos(turn), np.sin(turn)], 0).astype(np.float32)
 
 
@@ -42,11 +41,6 @@
 
 def dot_t(left, right):
     return lax.dot_general(left, right, (((1,), (1,)), ((), ())), preferred_element_type=F32)
-
-
-def halves(value):
-    high = value.astype(BF16)
-    return high, (value - high.astype(F32)).astype(BF16)
 
 
 def kernel(
@@ -182,7 +176,7 @@
     for j in range(3):
         tab_t[...] = tab_buf[j].T
         spec[pl.ds(32 * j, 32), 0:512] = tab_t[pl.ds(rows, 32), :].astype(F32)
-    table = spec[0:96, 0:512].astype(BF16)
+    table = jnp.concatenate([spec[0:96, 0:256], spec[0:96, 256:512]], 0).astype(BF16)
 
     def tok_x(k):
         line = tok_all.at[pl.ds(xy * 8, 8)]
@@ -194,19 +188,37 @@
         tok_x(k).start()
 
     def filt_over_x(wave, k):
-        spots = pl.ds(0, 5) if wave == 0 else pl.ds(5, 3)
+        spots = pl.ds(WAVES[wave], WAVES[wave + 1] - WAVES[wave])
         other = lax.rem(xy + k, 8)
         return remote(
             filt_z.at[other, spots], filt_x.at[xy, spots], fx_s.at[wave, k], fx_r.at[wave, k], xy_peer(k)
         )
 
+    def ring(direction, step):
+        which = lax.rem(z + (8 - step if direction > 0 else step), 8)
+        chunk = b_all.at[:, :, which] if step < 3 else b_all.at[:, 0 if direction > 0 else 1, which]
+        sems = (bp_s if direction > 0 else bm_s).at[step]
+        return remote(chunk, chunk, sems, b_r.at[direction, step], z_peer(1 if direction > 0 else 7))
+
+    def ring_on(step):
+        for direction in (1, 0):
+            ring(direction, step).wait()
+            if step < 3:
+                ring(direction, step + 1).start()
+
+    swap.wait()
+    ring(1, 0).start()
+    ring(0, 0).start()
+
     for k in range(1, 8):
         tok_x(k).wait()
 
     def embed(chunk, carry):
         ids = jnp.concatenate([tok_all[chunk * 4 + i] for i in range(4)], 1)
-        hot = (lax.broadcasted_iota(jnp.int32, (512, 512), 0) == ids).astype(F32).astype(BF16)
-        value = dot(table, hot)
+        upper = ids >= 256
+        hot = (lax.broadcasted_iota(jnp.int32, (256, 512), 0) == jnp.where(upper, ids - 256, ids))
+        both = dot(table, hot.astype(F32).astype(BF16))
+        value = jnp.where(upper, both[96:], both[:96])
         wide = jnp.concatenate([carry, value], 1)
         total = None
         parts = []
@@ -223,71 +235,53 @@
             query[at, :] = parts[0][:, i * 128 : (i + 1) * 128]
         return value[:, 384:]
 
+    def wave_on(wave):
+        for k in NEAR[max(1, WAVES[wave]) : WAVES[wave + 1]]:
+            filt_along_z(k).wait()
+        for k in range(1, 8):
+            filt_over_x(wave, k).start()
+
     carry = lax.fori_loop(0, 8, embed, jnp.zeros((96, 128), F32))
-    for k in NEAR[1:5]:
-        filt_along_z(k).wait()
-    for k in range(1, 8):
-        filt_over_x(0, k).start()
-    carry = lax.fori_loop(8, 16, embed, carry)
-    for k in NEAR[5:]:
-        filt_along_z(k).wait()
-    for k in range(1, 8):
-        filt_over_x(1, k).start()
+    wave_on(0)
+    lax.fori_loop(8, 16, embed, carry)
+    wave_on(1)
+    wave_on(2)
     filt_x[xy] = filt_z[xy]
-
-    def ring(direction, step):
-        which = lax.rem(z + (8 - step if direction > 0 else step), 8)
-        chunk = b_all.at[:, :, which] if step < 3 else b_all.at[:, 0 if direction > 0 else 1, which]
-        sems = (bp_s if direction > 0 else bm_s).at[step]
-        return remote(chunk, chunk, sems, b_r.at[direction, step], z_peer(1 if direction > 0 else 7))
-
-    def ring_on(step):
-        for direction in (1, 0):
-            ring(direction, step).wait()
-            if step < 3:
-                ring(direction, step + 1).start()
-
-    swap.wait()
-    ring(1, 0).start()
-    ring(0, 0).start()
 
     def first():
         return dft_ref[0:128, :]
 
     def last():
-        return jnp.concatenate([dft_ref[128 + 64 * i : 192 + 64 * i, :] for i in range(3)], 1)
-
-    def w_high():
-        return jnp.concatenate([dft_ref[320:576, :], dft_ref[576:832, :]], 1)
-
-    def w_low():
-        return jnp.concatenate([dft_ref[832:1088, :], dft_ref[1088:1344, :]], 1)
+        return jnp.concatenate([dft_ref[128:192, :], dft_ref[192:256, :]], 1)
+
+    def inner():
+        return jnp.concatenate([dft_ref[256:512, :], dft_ref[512:768, :]], 1)
 
     def turns():
         return turn_ref[0:64, :], turn_ref[64:128, :]
 
     def forward(source, group):
-        columns = [source[pl.ds(group * 4 + i, 64, stride=32), :] for i in range(4)]
+        columns = [source[pl.ds(group * 8 + i, 64, stride=32), :] for i in range(8)]
         column = jnp.concatenate(columns, 1).astype(BF16)
         stage = dot(first(), jnp.concatenate([column, column], 0))
         cos, sin = turns()
         turned_rows = []
-        for i in range(4):
+        for i in range(8):
             re, im = stage[:64, i * 128 : (i + 1) * 128], stage[64:, i * 128 : (i + 1) * 128]
             turned_rows.append(jnp.concatenate([re * cos + im * sin, im * cos - re * sin], 1))
-        high, low = halves(jnp.concatenate(turned_rows, 0))
-        return dot(high, w_high()) + (dot(low, w_high()) + dot(high, w_low()))
+        return dot(jnp.concatenate(turned_rows, 0).astype(BF16), inner())
 
     def signal_side(group, _):
-        spec[pl.ds(pl.multiple_of(group * 256, 256), 256), 0:256] = forward(gated, group)
+        spec[pl.ds(pl.multiple_of(group * 512, 512), 512), 0:256] = forward(gated, group)
         return 0
 
-    lax.fori_loop(0, 8, signal_side, 0)
+    lax.fori_loop(0, 4, signal_side, 0)
     for k in range(1, 8):
         filt_over_x(0, k).wait()
     ring_on(0)
-    for k in range(1, 8):
-        filt_over_x(1, k).wait()
+    for wave in (1, 2):
+        for k in range(1, 8):
+            filt_over_x(wave, k).wait()
     for other in range(8):
         for spot in range(8):
             from_z = lax.rem(z + 8 - NEAR[spot], 8)
@@ -296,22 +290,22 @@
 
     def filter_side(group, _):
         h = forward(filt_f, group)
-        s = spec[pl.ds(pl.multiple_of(group * 256, 256), 256), 0:256]
+        s = spec[pl.ds(pl.multiple_of(group * 512, 512), 512), 0:256]
         sr, si, hr, hi = s[:, :128], s[:, 128:], h[:, :128], h[:, 128:]
-        high, low = halves(jnp.concatenate([sr * hr - si * hi, sr * hi + si * hr], 1))
-        back = dot_t(high, w_high()) + (dot_t(low, w_high()) + dot_t(high, w_low()))
+        product = jnp.concatenate([sr * hr - si * hi, sr * hi + si * hr], 1).astype(BF16)
+        back = dot_t(product, inner())
         cos, sin = turns()
         parts = []
-        for i in range(4):
+        for i in range(8):
             re, im = back[i * 64 : (i + 1) * 64, :128], back[i * 64 : (i + 1) * 64, 128:]
             parts.append(jnp.concatenate([re * cos - im * sin, im * cos + re * sin], 0))
-        high, low = halves(jnp.concatenate(parts, 1))
-        result = dot(last(), jnp.concatenate([high, low, high], 0)) * (1.0 / 8192)
-        for i in range(4):
-            long_f[pl.ds(group * 4 + i, 64, stride=32), :] = result[:, i * 128 : (i + 1) * 128]
+        column = jnp.concatenate(parts, 1).astype(BF16)
+        result = dot(last(), jnp.concatenate([column, column], 0)) * (1.0 / 8192)
+        for i in range(8):
+            long_f[pl.ds(group * 8 + i, 64, stride=32), :] = result[:, i * 128 : (i + 1) * 128]
         return 0
 
-    lax.fori_loop(0, 8, filter_side, 0)
+    lax.fori_loop(0, 4, filter_side, 0)
 
     skip = jnp.broadcast_to(tin[:, 9:10], (32, 128))
     for index in range(64):
@@ -342,11 +336,15 @@
             a_x(t, right).wait()
             a_on(t, right).start()
 
-    for t in range(4):
+    def start_a_z(t):
         for k in NEAR[1:]:
             a_z(t, k).start()
         all_a[x, order[t], :, z] = send_a[order[t], :, z]
+
+    start_a_z(0)
+    start_a_z(1)
     ring_on(1)
+    start_a_z(2)
 
     def c_core(t):
         return remote(c_send.at[t], c_recv.at[t], cc_s.at[t], cc_r.at[t], core_peer)
@@ -363,17 +361,15 @@
         else:
             c_mine[t] = total
 
-    for t in range(4):
+    def z_to_x(t):
         for k in NEAR[1:]:
             a_z(t, k).wait()
         for right in (1, 0):
             a_x(t, right).start()
         if t > 0:
             pass_on(t - 1)
-    ring_on(2)
-    pass_on(3)
-    ring_on(3)
-    for t in range(4):
+
+    def multiply(t):
         for right in (1, 0):
             a_on(t, right).wait()
 
@@ -385,6 +381,7 @@
                 weights = b_all[part].reshape(256, 1024)[:, xs * 256 : (xs + 1) * 256]
                 term = dot(weights, jnp.concatenate(blocks, 1))
                 total = term if total is None else total + term
+
             @pl.when(core == 0)
             def _():
                 c_mine[t, at, :] = total[:, :128]
@@ -399,8 +396,22 @@
 
         lax.fori_loop(0, 3, columns, 0)
         c_core(t).start()
-        if t > 0:
-            after_core(t - 1)
+
+    z_to_x(0)
+    z_to_x(1)
+    ring_on(2)
+    start_a_z(3)
+    z_to_x(2)
+    z_to_x(3)
+    ring_on(3)
+    multiply(0)
+    multiply(1)
+    after_core(0)
+    pass_on(3)
+    multiply(2)
+    after_core(1)
+    multiply(3)
+    after_core(2)
     after_core(3)
     for t in range(3):
         c_y(t).wait()
@@ -497,7 +508,7 @@
         pltpu.VMEM((128, 256), BF16),
         pltpu.VMEM((128, 256), BF16),
         dma, dma((8,)), dma((8,)), dma((8,)), dma((8,)),
-        dma((8,)), dma((8,)), dma((2, 8)), dma((2, 8)),
+        dma((8,)), dma((8,)), dma((3, 8)), dma((3, 8)),
         dma, dma, dma((4,)), dma((4,)), dma((2, 4)),
         dma((4, 8)), dma((4, 8)), dma((4, 4)), dma((4, 4)),
         dma((4,)), dma((4,)), dma((3,)), dma((3,)),

time: 88.8 us -> 80.2 us (0.903)
  Pallas kernels: 86.9 us -> 78.1 us
    pallas_call x1, Pallas kernels: 86.9 us -> 78.1 us  [per_device(): pl.pallas_call(kernel, out_shape=jax.ShapeDtypeStruct((128, 256), BF16),...]
where the time goes in v3:
time: 80.2 us; the launch traced here: 79.6 us
  Pallas kernels  78.1 us (97%)
  local copies, waits for them, and re-layouts  1.47 us (2%)
    pallas_call x1, Pallas kernels, per_device(): pl.pallas_call(kernel, out_shape=jax.ShapeDtypeStruct((128, 256), BF16),...  78.1 us

profile of v3, /device:TPU:6, one launch (start us, length us, event | category | flops | bytes accessed | tf_op | source)
XLA Modules:
  0.0 79.6 jit_solution(3416230335033765774)
XLA Ops:
  0.0 78.1 %shard_map.109 = bf16[128,256]{1,0:T(8,128)(2,1)} custom-call(s32[1,128]{1,0:T(1,128)} %bitcast.9, bf16[3,512,2048]{2,1,0:T(8,128)(2,1)} %bitcast.5, bf16[128,2048]{1,0:T(8,128)(2,1)} %filt_hbm.1, f32[3,3,2048]{2,1,0:T(4,128)} %tin_hbm.1, f32[16,128]{1,0:T(8,128)} %bitcast.7, bf16[3,16,2048]{2,1,0:T(8,128)(2,1)} %bitcast.6, f32[3,3,256]{2,1,0:T(4,128)} %tpr_hbm.1, ...), custom_call_target="tpu_custom_call" | custom-call | tf_op jit(solution)/shard_map/pallas_call | solution.py:517
  78.1 1.5 %copy.13 = bf16[128,256]{1,0:T(8,128)(2,1)} copy(bf16[128,256]{1,0:T(8,128)(2,1)} %shard_map.109) | data formatting | bytes 131072

commit v4 on v3

--- a/solution.py
+++ b/solution.py
@@ -54,6 +54,7 @@
     taps_mine, halo_send, halo_recv, out_send, out_recv,
     tab_sem, tz_s, tz_r, tx_s, tx_r, fz_s, fz_r, fx_s, fx_r, sw_s, sw_r, bp_s, bm_s, b_r,
     az_s, az_r, ax_s, ax_r, cc_s, cc_r, cy_s, cy_r, tp_s, tp_r, h_s, h_r, o_s, o_r,
+    lz_s, lz_r, lx_s, lx_r,
 ):
     ctx, ch = lax.axis_index("ctx"), lax.axis_index("ch")
     x, yl, z = ctx // 16, (ctx // 8) % 2, ctx % 8
@@ -127,13 +128,30 @@
         for part in range(4):
             index = group * 4 + part
             filt_t[index // 8, index % 8] = block[part * 32 : (part + 1) * 32]
-    for load in loads[1:]:
+    loads[1].wait()
+    tok_all[ctx] = tok_ref[...]
+    expected = 17 + jnp.where(is_turned, 1, 0)
+    expected += jnp.where((z == 7) & has_next, 1, 0) + jnp.where((z == 0) & has_prev, 1, 0)
+    pl.semaphore_wait(bar, expected)
+
+    def tok_z(k):
+        return remote(tok_all.at[ctx], tok_all.at[ctx], tz_s.at[k], tz_r.at[k], z_peer(k))
+
+    def filt_along_z(k):
+        return remote(
+            filt_t.at[:, lax.rem(z + k, 8)], filt_z.at[:, SPOT[k]], fz_s.at[k], fz_r.at[k], z_peer(k)
+        )
+
+    for k in range(1, 8):
+        tok_z(k).start()
+    for k in NEAR[1:]:
+        filt_along_z(k).start()
+    for load in loads[2:]:
         load.wait()
     for half in range(2):
         for part in range(4):
             start = part * 512 + half * 256
             b_half[half, :, :, part * 256 : (part + 1) * 256] = proj_ref[:, :, start : start + 256]
-    tok_all[ctx] = tok_ref[...]
     stacked = [tin_ref[s, :, pl.ds(lanes, 128)] for s in range(3)] + [skip_ref[pl.ds(ctx // 4, 1), :]]
     tin_t[...] = jnp.concatenate(stacked + [jnp.zeros((6, 128), F32)], 0).T
     for s in range(3):
@@ -144,22 +162,6 @@
     rows = pl.multiple_of((ctx % 4) * 32, 32)
     tin = tin_t[pl.ds(rows, 32), :]
 
-    expected = 17 + jnp.where(is_turned, 1, 0)
-    expected += jnp.where((z == 7) & has_next, 1, 0) + jnp.where((z == 0) & has_prev, 1, 0)
-    pl.semaphore_wait(bar, expected)
-
-    def tok_z(k):
-        return remote(tok_all.at[ctx], tok_all.at[ctx], tz_s.at[k], tz_r.at[k], z_peer(k))
-
-    def filt_along_z(k):
-        return remote(
-            filt_t.at[:, lax.rem(z + k, 8)], filt_z.at[:, SPOT[k]], fz_s.at[k], fz_r.at[k], z_peer(k)
-        )
-
-    for k in range(1, 8):
-        tok_z(k).start()
-    for k in NEAR[1:]:
-        filt_along_z(k).start()
     swap = remote(b_half.at[1 - yl], b_all.at[:, yl, z], sw_s, sw_r, dev(x, 1 - yl, z, ch))
     swap.start()
     taps_copy = remote(tout_ref, taps_mine, tp_s, tp_r, turned)
@@ -341,6 +343,37 @@
             a_z(t, k).start()
         all_a[x, order[t], :, z] = send_a[order[t], :, z]
 
+    def last_block(part):
+        return 1 - core if part == 0 else core
+
+    def last_z(part, k):
+        return remote(
+            send_a.at[order[3], last_block(part), lax.rem(z + k, 8)],
+            all_a.at[x, order[3], last_block(part), z],
+            lz_s.at[part, k], lz_r.at[part, k], z_peer(k),
+        )
+
+    def last_x(part, k):
+        mine = all_a.at[x, order[3], last_block(part)]
+        return remote(mine, mine, lx_s.at[part, k], lx_r.at[part, k], x_peer(k))
+
+    def start_last_z(part):
+        for k in NEAR[1:]:
+            last_z(part, k).start()
+        all_a[x, order[3], last_block(part), z] = send_a[order[3], last_block(part), z]
+
+    def last_z_to_x(part):
+        for k in NEAR[1:]:
+            last_z(part, k).wait()
+        for k in (1, 3, 2):
+            last_x(part, k).start()
+
+    def last_multiply(part):
+        for k in (1, 3, 2):
+            last_x(part, k).wait()
+        block = jnp.concatenate([all_a[xs, order[3], last_block(part)].reshape(256, 128) for xs in range(4)], 0)
+        return dot(b_all[...].reshape(768, 1024), block)
+
     start_a_z(0)
     start_a_z(1)
     ring_on(1)
@@ -355,107 +388,111 @@
     def after_core(t):
         c_core(t).wait()
         total = c_mine[t] + c_recv[t].astype(F32)
-        if t < 3:
-            y_send[t] = total.astype(BF16)
-            c_y(t).start()
-        else:
-            c_mine[t] = total
+        y_send[t] = total.astype(BF16)
+        c_y(t).start()
 
     def z_to_x(t):
         for k in NEAR[1:]:
             a_z(t, k).wait()
         for right in (1, 0):
             a_x(t, right).start()
-        if t > 0:
-            pass_on(t - 1)
 
     def multiply(t):
         for right in (1, 0):
             a_on(t, right).wait()
 
-        def columns(part, _):
-            at = pl.ds(pl.multiple_of(part * 256, 256), 256)
-            total = None
-            for xs in range(4):
-                blocks = [all_a[xs, order[t], lo].reshape(256, 128) for lo in range(2)]
-                weights = b_all[part].reshape(256, 1024)[:, xs * 256 : (xs + 1) * 256]
-                term = dot(weights, jnp.concatenate(blocks, 1))
-                total = term if total is None else total + term
-
-            @pl.when(core == 0)
-            def _():
-                c_mine[t, at, :] = total[:, :128]
-                c_send[t, at, :] = total[:, 128:].astype(BF16)
-
-            @pl.when(core == 1)
-            def _():
-                c_mine[t, at, :] = total[:, 128:]
-                c_send[t, at, :] = total[:, :128].astype(BF16)
-
-            return 0
-
-        lax.fori_loop(0, 3, columns, 0)
+        total = None
+        for xs in range(4):
+            blocks = [all_a[xs, order[t], lo].reshape(256, 128) for lo in range(2)]
+            weights = b_all[...].reshape(768, 1024)[:, xs * 256 : (xs + 1) * 256]
+            term = dot(weights, jnp.concatenate(blocks, 1))
+            total = term if total is None else total + term
+
+        @pl.when(core == 0)
+        def _():
+            c_mine[t] = total[:, :128]
+            c_send[t] = total[:, 128:].astype(BF16)
+
+        @pl.when(core == 1)
+        def _():
+            c_mine[t] = total[:, 128:]
+            c_send[t] = total[:, :128].astype(BF16)
+
         c_core(t).start()
 
     z_to_x(0)
     z_to_x(1)
+    pass_on(0)
     ring_on(2)
-    start_a_z(3)
+    start_last_z(0)
+    start_last_z(1)
     z_to_x(2)
-    z_to_x(3)
+    pass_on(1)
     ring_on(3)
     multiply(0)
+    pass_on(2)
     multiply(1)
     after_core(0)
-    pass_on(3)
+    last_z_to_x(0)
+    after_core(1)
+    last_z_to_x(1)
     multiply(2)
-    after_core(1)
-    multiply(3)
+    c_send[3] = last_multiply(0).astype(BF16)
+    c_core(3).start()
     after_core(2)
-    after_core(3)
+    summed = last_multiply(1)
+    c_core(3).wait()
+    summed += c_recv[3].astype(F32)
     for t in range(3):
         c_y(t).wait()
-    summed = c_mine[3] + y_recv[0].astype(F32) + y_recv[1].astype(F32) + y_recv[2].astype(F32)
+        summed += y_recv[t].astype(F32)
     projected = jnp.concatenate([summed[i * 128 : (i + 1) * 128].T for i in range(6)], 1).astype(BF16)
 
     halo = remote(halo_send, halo_recv, h_s, h_r, owner(place + 1))
     halo_send[...] = projected[112:]
     pl.when(has_next)(lambda: halo.start())
 
+    pl.when(is_turned)(lambda: taps_copy.wait())
+
+    def shifted(value, s):
+        return value if s == 0 else pltpu.roll(value, s, 0)
+
+    def mix(wide):
+        feats = []
+        for j in range(3):
+            part = wide[:, j * 256 : (j + 1) * 256].astype(F32)
+            total = None
+            for s in range(3):
+                term = taps_mine[3 * s + j : 3 * s + j + 1, :] * shifted(part, s)
+                total = term if total is None else total + term
+            feats.append(total)
+        gate = feats[1] * feats[2]
+        short = None
+        for s in range(7):
+            term = taps_mine[9 + s : 10 + s, :] * shifted(gate, s)
+            short = term if short is None else short + term
+        return (feats[0] * (short + taps_mine[16:17, :] * gate))[16:].astype(BF16)
+
+    def out_copy(part):
+        at = (pl.ds(16, 112), pl.ds(0, 16))[part]
+        return remote(out_send.at[at], out_recv.at[at], o_s.at[part], o_r.at[part], turned)
+
+    out_send[16:] = mix(projected)
+    pl.when(is_turned)(lambda: out_copy(0).start())
+
     @pl.when(place == 0)
     def _():
         halo_recv[...] = jnp.zeros_like(halo_recv)
 
     pl.when(has_next)(lambda: halo.wait_send())
     pl.when(has_prev)(lambda: halo.wait_recv())
-    pl.when(is_turned)(lambda: taps_copy.wait())
-    wide = jnp.concatenate([halo_recv[...], projected], 0).astype(F32)
-
-    def shifted(value, s):
-        return value if s == 0 else pltpu.roll(value, s, 0)
-
-    feats = []
-    for j in range(3):
-        part = wide[:, j * 256 : (j + 1) * 256]
-        total = None
-        for s in range(3):
-            term = taps_mine[3 * s + j : 3 * s + j + 1, :] * shifted(part, s)
-            total = term if total is None else total + term
-        feats.append(total)
-    gate = feats[1] * feats[2]
-    short = None
-    for s in range(7):
-        term = taps_mine[9 + s : 10 + s, :] * shifted(gate, s)
-        short = term if short is None else short + term
-    mixed = (feats[0] * (short + taps_mine[16:17, :] * gate))[16:].astype(BF16)
-
-    out_send[...] = mixed
-    out_copy = remote(out_send, out_recv, o_s, o_r, turned)
+    out_send[0:16] = mix(jnp.concatenate([halo_recv[...], projected[:16]], 0))
 
     @pl.when(is_turned)
     def _():
-        out_copy.start()
-        out_copy.wait()
+        out_copy(1).start()
+        out_copy(0).wait()
+        out_copy(1).wait()
 
     @pl.when(x == ch)
     def _():
@@ -510,9 +547,10 @@
         dma, dma((8,)), dma((8,)), dma((8,)), dma((8,)),
         dma((8,)), dma((8,)), dma((3, 8)), dma((3, 8)),
         dma, dma, dma((4,)), dma((4,)), dma((2, 4)),
-        dma((4, 8)), dma((4, 8)), dma((4, 4)), dma((4, 4)),
+        dma((3, 8)), dma((3, 8)), dma((3, 4)), dma((3, 4)),
         dma((4,)), dma((4,)), dma((3,)), dma((3,)),
-        dma, dma, dma, dma, dma, dma,
+        dma, dma, dma, dma, dma((2,)), dma((2,)),
+        dma((2, 8)), dma((2, 8)), dma((2, 4)), dma((2, 4)),
     ]
     return pl.pallas_call(
         kernel,

time: 80.2 us -> 78.3 us (0.976)
  Pallas kernels: 78.1 us -> 76.7 us
    pallas_call x1, Pallas kernels: 78.1 us -> 76.7 us  [per_device(): pl.pallas_call(kernel, out_shape=jax.ShapeDtypeStruct((128, 256), BF16),...]
where the time goes in v4:
time: 78.3 us; the launch traced here: 78.2 us
  Pallas kernels  76.7 us (98%)
  local copies, waits for them, and re-layouts  1.47 us (2%)
    pallas_call x1, Pallas kernels, per_device(): pl.pallas_call(kernel, out_shape=jax.ShapeDtypeStruct((128, 256), BF16),...  76.7 us

profile of v4, /device:TPU:6, one launch (start us, length us, event | category | flops | bytes accessed | tf_op | source)
XLA Modules:
  0.0 78.2 jit_solution(11292885374005620009)
XLA Ops:
  0.0 76.7 %shard_map.109 = bf16[128,256]{1,0:T(8,128)(2,1)} custom-call(s32[1,128]{1,0:T(1,128)} %bitcast.9, bf16[3,512,2048]{2,1,0:T(8,128)(2,1)} %bitcast.5, bf16[128,2048]{1,0:T(8,128)(2,1)} %filt_hbm.1, f32[3,3,2048]{2,1,0:T(4,128)} %tin_hbm.1, f32[16,128]{1,0:T(8,128)} %bitcast.7, bf16[3,16,2048]{2,1,0:T(8,128)(2,1)} %bitcast.6, f32[3,3,256]{2,1,0:T(4,128)} %tpr_hbm.1, ...), custom_call_target="tpu_custom_call" | custom-call | tf_op jit(solution)/shard_map/pallas_call | solution.py:555
  76.7 1.5 %copy.13 = bf16[128,256]{1,0:T(8,128)(2,1)} copy(bf16[128,256]{1,0:T(8,128)(2,1)} %shard_map.109) | data formatting | bytes 131072

commit v5 on v4

--- a/solution.py
+++ b/solution.py
@@ -103,9 +103,7 @@
         (dft_hbm, dft_ref), (turn_hbm, turn_ref),
     )
     loads = [pltpu.make_async_copy(src, dst, load_sem.at[i]) for i, (src, dst) in enumerate(pairs)]
-    for load in loads:
-        load.start()
-    tab_copy.start()
+    loads[0].start()
 
     bar = pltpu.get_barrier_semaphore()
 
@@ -122,6 +120,9 @@
     pl.when((z == 7) & has_next)(lambda: greet(owner(place + 1)))
     pl.when((z == 0) & has_prev)(lambda: greet(owner(place - 1)))
 
+    for load in loads[1:]:
+        load.start()
+    tab_copy.start()
     loads[0].wait()
     for group in range(16):
         block = filt_ref[:, group * 128 : (group + 1) * 128].T
@@ -245,8 +246,9 @@
 
     carry = lax.fori_loop(0, 8, embed, jnp.zeros((96, 128), F32))
     wave_on(0)
-    lax.fori_loop(8, 16, embed, carry)
+    carry = lax.fori_loop(8, 12, embed, carry)
     wave_on(1)
+    lax.fori_loop(12, 16, embed, carry)
     wave_on(2)
     filt_x[xy] = filt_z[xy]
 
@@ -377,7 +379,6 @@
     start_a_z(0)
     start_a_z(1)
     ring_on(1)
-    start_a_z(2)
 
     def c_core(t):
         return remote(c_send.at[t], c_recv.at[t], cc_s.at[t], cc_r.at[t], core_peer)
@@ -421,21 +422,22 @@
         c_core(t).start()
 
     z_to_x(0)
+    start_a_z(2)
     z_to_x(1)
     pass_on(0)
     ring_on(2)
     start_last_z(0)
     start_last_z(1)
+    pass_on(1)
     z_to_x(2)
-    pass_on(1)
     ring_on(3)
     multiply(0)
+    multiply(1)
     pass_on(2)
-    multiply(1)
+    last_z_to_x(0)
     after_core(0)
-    last_z_to_x(0)
+    last_z_to_x(1)
     after_core(1)
-    last_z_to_x(1)
     multiply(2)
     c_send[3] = last_multiply(0).astype(BF16)
     c_core(3).start()

time: 78.3 us -> 77.9 us (level)
  no operation moved by 1% of the time
where the time goes in v5:
time: 77.9 us; the launch traced here: 77.7 us
  Pallas kernels  76.2 us (98%)
  local copies, waits for them, and re-layouts  1.47 us (2%)
    pallas_call x1, Pallas kernels, per_device(): pl.pallas_call(kernel, out_shape=jax.ShapeDtypeStruct((128, 256), BF16),...  76.2 us

profile of v5, /device:TPU:6, one launch (start us, length us, event | category | flops | bytes accessed | tf_op | source)
XLA Modules:
  0.0 77.7 jit_solution(6661092670092645943)
XLA Ops:
  0.0 76.2 %shard_map.109 = bf16[128,256]{1,0:T(8,128)(2,1)} custom-call(s32[1,128]{1,0:T(1,128)} %bitcast.9, bf16[3,512,2048]{2,1,0:T(8,128)(2,1)} %bitcast.5, bf16[128,2048]{1,0:T(8,128)(2,1)} %filt_hbm.1, f32[3,3,2048]{2,1,0:T(4,128)} %tin_hbm.1, f32[16,128]{1,0:T(8,128)} %bitcast.7, bf16[3,16,2048]{2,1,0:T(8,128)(2,1)} %bitcast.6, f32[3,3,256]{2,1,0:T(4,128)} %tpr_hbm.1, ...), custom_call_target="tpu_custom_call" | custom-call | tf_op jit(solution)/shard_map/pallas_call | solution.py:557
  76.3 1.5 %copy.13 = bf16[128,256]{1,0:T(8,128)(2,1)} copy(bf16[128,256]{1,0:T(8,128)(2,1)} %shard_map.109) | data formatting | bytes 131072

commit v6 on v5

--- a/solution.py
+++ b/solution.py
@@ -527,10 +527,10 @@
         pltpu.VMEM((8, 8, 32, 128), BF16),
         pltpu.VMEM((8, 8, 32, 128), BF16),
         pltpu.VMEM((8, 8, 32, 128), BF16),
-        pltpu.VMEM((2048, 128), F32),
-        pltpu.VMEM((2048, 128), F32),
-        pltpu.VMEM((2048, 128), F32),
-        pltpu.VMEM((2048, 128), F32),
+        pltpu.VMEM((2080, 128), F32),
+        pltpu.VMEM((2080, 128), F32),
+        pltpu.VMEM((2080, 128), F32),
+        pltpu.VMEM((2080, 128), F32),
         pltpu.VMEM((2048, 512), F32),
         pltpu.VMEM((4, 2, 8, 32, 128), BF16),
         pltpu.VMEM((4, 4, 2, 8, 32, 128), BF16),

time: 77.9 us -> 77.9 us (level)
  no operation moved by 1% of the time
where the time goes in v6:
time: 77.9 us; the launch traced here: 77.7 us
  Pallas kernels  76.2 us (98%)
  local copies, waits for them, and re-layouts  1.47 us (2%)
    pallas_call x1, Pallas kernels, per_device(): pl.pallas_call(kernel, out_shape=jax.ShapeDtypeStruct((128, 256), BF16),...  76.2 us

profile of v6, /device:TPU:6, one launch (start us, length us, event | category | flops | bytes accessed | tf_op | source)
XLA Modules:
  0.0 77.7 jit_solution(17258687014718228861)
XLA Ops:
  0.0 76.2 %shard_map.109 = bf16[128,256]{1,0:T(8,128)(2,1)} custom-call(s32[1,128]{1,0:T(1,128)} %bitcast.9, bf16[3,512,2048]{2,1,0:T(8,128)(2,1)} %bitcast.5, bf16[128,2048]{1,0:T(8,128)(2,1)} %filt_hbm.1, f32[3,3,2048]{2,1,0:T(4,128)} %tin_hbm.1, f32[16,128]{1,0:T(8,128)} %bitcast.7, bf16[3,16,2048]{2,1,0:T(8,128)(2,1)} %bitcast.6, f32[3,3,256]{2,1,0:T(4,128)} %tpr_hbm.1, ...), custom_call_target="tpu_custom_call" | custom-call | tf_op jit(solution)/shard_map/pallas_call | solution.py:557
  76.3 1.5 %copy.13 = bf16[128,256]{1,0:T(8,128)(2,1)} copy(bf16[128,256]{1,0:T(8,128)(2,1)} %shard_map.109) | data formatting | bytes 131072
